TPU v7x, 256 devices: a whole 4x4x8 slice. The times are simulated.
256 devices in a mesh: dp: 32 (over z, x), mp: 8 (over y, core).
Axes of the slice: x: 4, y: 4, z: 8, core: 2. Of those that a mesh axis runs over, the one named last changes fastest.
Arguments:
- gradient: bfloat16 [4, 8192, 8192], P(None, 'dp', 'mp')
- owners: int32 [256], replicated, may hold values from 0 to 31, as said below
- left_basis: bfloat16 [256, 1024, 1024], P(('dp', 'mp')), may hold values from -0.1875 to 0.1875
- right_basis: bfloat16 [256, 1024, 1024], P(('dp', 'mp')), may hold values from -0.1875 to 0.1875
- first_moment: bfloat16 [256, 1024, 1024], P(('dp', 'mp')), may hold values from -0.1796875 to 0.1796875
- second_moment: bfloat16 [256, 1024, 1024], P(('dp', 'mp')), may hold values from 1.9907951e-05 to 0.00019931793
Outputs:
- update: bfloat16 [4, 8192, 8192], P(None, 'dp', 'mp')
Inputs may be any that keep to these rules, and one draw needn't show every extreme that they name: owners[t] is the data index of the device that owns tile t, whose model index is t mod 8; the tiles of one model index have distinct owners.
All inputs are finite; a program needn't handle non-finite values.
Results may differ from a plain program's by a relative error of at most 0.019.
Values may be sent and summed in bfloat16 or wider, within the bound.
A program may use at most 64 MiB of HBM per device.

v0:
```python
import math

import jax
import jax.numpy as jnp
from jax import lax
from jax.sharding import PartitionSpec as P

beta_one = 0.9
beta_two = 0.999
epsilon = 1e-08
correct_one = 1.0 - 0.9**3
correct_two = 1.0 - 0.999**3
clip_rms = 0.25


def per_device(gradient, owners, left_basis, right_basis, first_moment, second_moment):
    data_size = lax.axis_size("dp")
    model_size = lax.axis_size("mp")
    quarters, row_part, block_size = gradient.shape
    groups = data_size // quarters
    left_tile = left_basis[0]
    right_tile = right_basis[0]
    model_index = lax.axis_index("mp")
    owner_table = owners.reshape(data_size, model_size)
    column_owners = lax.dynamic_slice_in_dim(owner_table, model_index, 1, 1)[:, 0]
    tile_of_owner = (
        jnp.zeros((data_size,), jnp.int32)
        .at[column_owners]
        .set(jnp.arange(data_size, dtype=jnp.int32))
    )
    local_squares = jnp.sum(jnp.square(gradient.astype(jnp.float32)))
    total_squares = lax.psum(local_squares, ("dp", "mp"))
    width = block_size // data_size
    pieces = gradient.reshape(quarters, row_part, data_size, width)
    arrived = lax.all_to_all(pieces, "dp", split_axis=2, concat_axis=0, tiled=True)
    tiles = arrived.reshape(groups, quarters, quarters, row_part, width).transpose(2, 0, 1, 3, 4)
    tiles = tiles.reshape(data_size, block_size, width)
    outgoing = jnp.take(tiles, tile_of_owner, axis=0)
    received = lax.all_to_all(outgoing, "dp", split_axis=0, concat_axis=0, tiled=True)
    turned_part = lax.dot_general(
        left_tile, received, (((0,), (1,)), ((), ())), preferred_element_type=jnp.float32
    )
    column_sums = jnp.sum(jnp.square(received.astype(jnp.float32)), axis=1, keepdims=True)
    rotated, column_sums = (turned_part.astype(jnp.bfloat16), column_sums)
    rotated = rotated.reshape(block_size, block_size)
    tile_count = data_size * model_size
    clip_limit = clip_rms * math.sqrt(tile_count * block_size * block_size)
    factor = jnp.minimum(jnp.float32(1.0), clip_limit / jnp.sqrt(total_squares))
    turned = jnp.dot(rotated, right_tile, preferred_element_type=jnp.float32) * factor
    first_new = beta_one * first_moment[0].astype(jnp.float32) + (1.0 - beta_one) * turned
    second_new = (
        beta_two * second_moment[0].astype(jnp.float32) + (1.0 - beta_two) * turned * turned
    )
    step_rotated = (
        first_new / correct_one / (jnp.sqrt(second_new / correct_two) + epsilon)
    ).astype(jnp.bfloat16)
    back_columns = lax.dot_general(
        step_rotated, right_tile, (((1,), (1,)), ((), ())), preferred_element_type=jnp.float32
    )
    back_columns = back_columns.astype(jnp.bfloat16)
    result = jnp.dot(left_tile, back_columns, preferred_element_type=jnp.float32).astype(
        jnp.bfloat16
    )
    width = block_size // data_size
    back = lax.all_to_all(
        result.reshape(block_size, data_size, width), "dp", split_axis=1, concat_axis=1, tiled=True
    )
    by_tile = jnp.take(back, column_owners, axis=1)
    spread_out = by_tile.reshape(quarters, row_part, quarters, groups, width).transpose(
        3, 0, 2, 1, 4
    )
    spread_out = spread_out.reshape(data_size, quarters, row_part, width)
    returned = lax.all_to_all(spread_out, "dp", split_axis=0, concat_axis=3, tiled=True)
    return returned.reshape(quarters, row_part, block_size)


def solution(mesh):
    placed = (
        P(None, "dp", "mp"),
        P(),
        P(("dp", "mp"), None, None),
        P(("dp", "mp"), None, None),
        P(("dp", "mp"), None, None),
        P(("dp", "mp"), None, None),
    )
    return jax.shard_map(
        per_device, mesh=mesh, in_specs=placed, out_specs=P(None, "dp", "mp"), check_vma=False
    )
```

profile of v0, /device:TPU:8, one launch (start us, length us, event | category | flops | bytes accessed | tf_op | source)
XLA Modules:
  0.0 334.2 jit_solution(4619482785173453567)
XLA Ops:
  0.0 4.1 %copy.17 = bf16[4,256,1024]{1,2,0:T(8,128)(2,1)} copy(bf16[4,256,1024]{2,1,0:T(8,128)(2,1)} %param.6) | data formatting | bytes 4194304 | tf_op args[0]
  4.1 3.1 copy.18
  7.2 11.6 %all-to-all-start = ((bf16[4,256,32,32]{1,3,0,2:T(8,128)(2,1)}), bf16[4,256,32,32]{1,3,0,2:T(8,128)(2,1)}, u32[]{:S(2)}, u32[]{:S(2)}) async-start(bf16[4,256,32,32]{1,3,0,2:T(8,128)(2,1)} %copy.18), calls=%async_computation | async-start | bytes 4194304 | tf_op jit(solution)/shard_map/all_to_all | solution.py:35
  18.9 0.2 fusion.25
  19.1 0.7 scatter_custom_fusion
  19.8 49.1 %all-to-all-done = bf16[4,256,32,32]{1,3,0,2:T(8,128)(2,1)} async-done(((bf16[4,256,32,32]{1,3,0,2:T(8,128)(2,1)}), bf16[4,256,32,32]{1,3,0,2:T(8,128)(2,1)}, u32[]{:S(2)}, u32[]{:S(2)}) %all-to-all-start) | async-done | bytes 2097184 | tf_op jit(solution)/shard_map/all_to_all | solution.py:35
  68.9 4.9 %copy.25 = bf16[8,4,4,256,32]{3,1,4,0,2:T(4,128)(2,1)} copy(bf16[8,4,4,256,32]{3,4,2,1,0:T(8,128)(2,1)} %bitcast.4) | data formatting | bytes 4194304 | tf_op jit(solution)/shard_map/reshape | solution.py:36
  73.8 4.4 %reshape.48 = bf16[32,1024,32]{1,2,0:T(8,128)(2,1)} reshape(bf16[4,8,4,256,32]{3,2,4,1,0:T(4,128)(2,1)} %bitcast.67) | data formatting | bytes 4194304 | tf_op jit(solution)/shard_map/reshape | solution.py:37
  78.3 3.6 %gather_fusion = bf16[32,1024,32]{1,2,0:T(8,128)(2,1)} fusion(bf16[32,1024,32]{1,2,0:T(8,128)(2,1)} %reshape.48, s32[1024]{0:T(1024)S(1)} %pad_clamp_fusion.1), kind=kCustom, calls=%fused_computation | custom fusion | bytes 4194432 | tf_op jit(solution)/shard_map/jit(_take)/gather | solution.py:38
  81.8 3.2 broadcast_select_fusion
  85.0 6.1 %all-to-all-start.1 = ((bf16[32,1024,32]{1,2,0:T(8,128)(2,1)}), bf16[32,1024,32]{1,2,0:T(8,128)(2,1)}, u32[]{:S(2)}, u32[]{:S(2)}) async-start(bf16[32,1024,32]{1,2,0:T(8,128)(2,1)} %broadcast_select_fusion), calls=%async_computation.1 | async-start | bytes 4194304 | tf_op jit(solution)/shard_map/all_to_all | solution.py:39
  91.1 3.3 multiply_reduce_fusion
  94.4 87.8 %psum.7 = f32[]{:T(128)} all-reduce(f32[]{:T(128)} %multiply_reduce_fusion), channel_id=1, replica_groups=mesh['dp'=32,'mp'=8] {'dp','mp'}, use_global_device_ids=true, to_apply=%region_2.0 | all-reduce | flops 1 | bytes 8 | tf_op jit(solution)/shard_map/psum | solution.py:32
  182.8 5.2 %fusion.22 = bf16[32,32,1024]{2,1,0:T(8,128)(2,1)} fusion(bf16[32,1024,32]{1,2,0:T(8,128)(2,1)} %all-to-all-done.1, bf16[1,1024,1024]{2,1,0:T(8,128)(2,1)S(1)} %copy-done), kind=kOutput, calls=%fused_computation.25 | convolution fusion | flops 2148532224 | bytes 6291456 | tf_op jit(solution)/shard_map/dot_general | solution.py:40
  188.1 12.7 %fusion.7 = bf16[1024,1024]{1,0:T(8,128)(2,1)} fusion(bf16[1,1024,1024]{2,1,0:T(8,128)(2,1)} %param.9, bf16[1,1024,1024]{2,1,0:T(8,128)(2,1)} %param.11, bf16[1,1024,1024]{2,1,0:T(8,128)(2,1)} %param.10, bf16[1024,1024]{0,1:T(8,128)(2,1)} %bitcast.71, f32[]{:T(128)S(6)} %min_shard_map.3), kind=kOutput, calls=%fused_computation.13 | convolution fusion | flops 4310695936 | bytes 10485764 | tf_op jit(solution)/shard_map/dot_general | solution.py:57
  200.7 5.3 %fusion.17 = bf16[1024,1024]{1,0:T(8,128)(2,1)} fusion(bf16[1,1024,1024]{2,1,0:T(8,128)(2,1)S(1)} %copy-done, bf16[1024,1024]{1,0:T(8,128)(2,1)} %fusion.7), kind=kOutput, calls=%fused_computation.24 | convolution fusion | flops 2148532224 | bytes 6291456 | tf_op jit(solution)/shard_map/dot_general | solution.py:61
  206.0 7.7 %all-to-all-start.2 = ((bf16[1024,32,32]{0,2,1:T(8,128)(2,1)}), bf16[1024,32,32]{0,2,1:T(8,128)(2,1)}, u32[]{:S(2)}, u32[]{:S(2)}) async-start(bf16[1024,32,32]{0,2,1:T(8,128)(2,1)} %bitcast.70), calls=%async_computation.2 | async-start | bytes 4194304 | tf_op jit(solution)/shard_map/all_to_all | solution.py:65
  214.2 49.6 %all-to-all-done.2 = bf16[1024,32,32]{0,2,1:T(8,128)(2,1)} async-done(((bf16[1024,32,32]{0,2,1:T(8,128)(2,1)}), bf16[1024,32,32]{0,2,1:T(8,128)(2,1)}, u32[]{:S(2)}, u32[]{:S(2)}) %all-to-all-start.2) | async-done | bytes 2097184 | tf_op jit(solution)/shard_map/all_to_all | solution.py:65
  263.7 3.6 %gather_fusion.1 = bf16[32,1024,32]{1,2,0:T(8,128)(2,1)} fusion(bf16[1024,32,32]{0,2,1:T(8,128)(2,1)} %all-to-all-done.2, s32[1024]{0:T(1024)S(1)} %pad_clamp_fusion), kind=kCustom, calls=%fused_computation.1 | custom fusion | bytes 4194432 | tf_op jit(solution)/shard_map/jit(_take)/gather | solution.py:68
  267.3 4.5 %gather.12 = bf16[4,256,4,8,32]{1,0,4,3,2:T(4,128)(2,1)} reshape(bf16[1024,32,32]{0,2,1:T(8,128)(2,1)} %bitcast.65) | data formatting | bytes 4194304 | tf_op jit(solution)/shard_map/jit(_take)/gather | solution.py:68
  271.8 1.9 copy_select_fusion
  273.7 55.0 %all_to_all.40 = bf16[32,4,256,32]{2,3,1,0:T(8,128)(2,1)S(1)} all-to-all(bf16[32,4,256,32]{2,3,1,0:T(8,128)(2,1)S(1)} %bitcast.66), channel_id=1, replica_groups=mesh['dp'=32,'mp'=8] {'dp'}, dimensions={0} | all-to-all | bytes 4194304 | tf_op jit(solution)/shard_map/all_to_all | solution.py:73
  328.7 1.6 copy.21
  330.2 3.9 %copy.22 = bf16[4,256,1024]{2,1,0:T(8,128)(2,1)} copy(bf16[4,256,1024]{1,2,0:T(8,128)(2,1)} %bitcast.68) | data formatting | bytes 4194304 | tf_op jit(solution)/shard_map/reshape | solution.py:74
  (14 shorter events, 0.5 us)
Async XLA Ops:
  0.0 182.8 %copy-start = (bf16[1,1024,1024]{2,1,0:T(8,128)(2,1)S(1)}, bf16[1,1024,1024]{2,1,0:T(8,128)(2,1)}, u32[]{:S(2)}) copy-start(bf16[1,1024,1024]{2,1,0:T(8,128)(2,1)} %param.8) | copy-start | bytes 6291460
  7.2 11.6 %copy-start.1 = (s32[256]{0:T(256)S(1)}, s32[256]{0:T(256)}, u32[]{:S(2)}) copy-start(s32[256]{0:T(256)} %param.7) | copy-start | bytes 3076
  7.2 61.7 %all-to-all-start = ((bf16[4,256,32,32]{1,3,0,2:T(8,128)(2,1)}), bf16[4,256,32,32]{1,3,0,2:T(8,128)(2,1)}, u32[]{:S(2)}, u32[]{:S(2)}) async-start(bf16[4,256,32,32]{1,3,0,2:T(8,128)(2,1)} %copy.18), calls=%async_computation | async-start | bytes 4194304 | tf_op jit(solution)/shard_map/all_to_all | solution.py:35
  85.0 97.8 %all-to-all-start.1 = ((bf16[32,1024,32]{1,2,0:T(8,128)(2,1)}), bf16[32,1024,32]{1,2,0:T(8,128)(2,1)}, u32[]{:S(2)}, u32[]{:S(2)}) async-start(bf16[32,1024,32]{1,2,0:T(8,128)(2,1)} %broadcast_select_fusion), calls=%async_computation.1 | async-start | bytes 4194304 | tf_op jit(solution)/shard_map/all_to_all | solution.py:39
  206.0 57.7 %all-to-all-start.2 = ((bf16[1024,32,32]{0,2,1:T(8,128)(2,1)}), bf16[1024,32,32]{0,2,1:T(8,128)(2,1)}, u32[]{:S(2)}, u32[]{:S(2)}) async-start(bf16[1024,32,32]{0,2,1:T(8,128)(2,1)} %bitcast.70), calls=%async_computation.2 | async-start | bytes 4194304 | tf_op jit(solution)/shard_map/all_to_all | solution.py:65
where the time goes:
time: 337 us; the launch traced here: 334 us
  blocking collectives  143 us (42%)
  waiting for transfers between devices  98.7 us (29%)
  local copies, waits for them, and re-layouts  34.6 us (10%)
  starting transfers between devices  25.4 us (8%)
  matrix products  23.2 us (7%)
  other arithmetic  8.75 us (3%)
    psum x1, blocking collectives, per_device(): total_squares = lax.psum(local_squares, ('dp', 'mp'))  87.8 us
    all_to_all x1, blocking collectives, per_device(): lax.all_to_all(spread_out, 'dp', split_axis=0, concat_axis=3, tiled=True)  55 us
    all_to_all x1, waiting for transfers between devices, per_device(): lax.all_to_all(result.reshape(block_size, data_size, width), 'dp', split_...  49.6 us
    all_to_all x1, waiting for transfers between devices, per_device(): lax.all_to_all(pieces, 'dp', split_axis=2, concat_axis=0, tiled=True)  49.1 us
    dot_general x1, matrix products, per_device(): lax.dot_general(step_rotated, right_tile, (((1,), (1,)), ((), ())), prefe...  12.7 us
    all_to_all x1, starting transfers between devices, per_device(): lax.all_to_all(pieces, 'dp', split_axis=2, concat_axis=0, tiled=True)  11.6 us
    gather x2, local copies, waits for them, and re-layouts, per_device(): by_tile = jnp.take(back, column_owners, axis=1)  8.09 us
    all_to_all x1, starting transfers between devices, per_device(): lax.all_to_all(result.reshape(block_size, data_size, width), 'dp', split_...  7.73 us
  transfers between devices with their start and end apart: 3, of which 2 were waited for; matrix products, arithmetic and copies ran while one was open for 1% of the time, Pallas kernels for 0%

commit v1 on v0

v1 whole, which is shorter than its diff:
```python
import functools
import math

import jax
import jax.numpy as jnp
from jax import lax
from jax.experimental import pallas as pl
from jax.experimental.pallas import tpu as pltpu
from jax.sharding import PartitionSpec as P

MESH = pl.DeviceIdType.MESH
B = 1024
S = 4
NZ, NX, NM = 8, 4, 8
ND = NZ * NX
Q = B // NX
H = Q // NZ
C = 4
W = B // C
T = 256

beta_one = 0.9
beta_two = 0.999
epsilon = 1e-08
correct_one = 1.0 - 0.9**3
correct_two = 1.0 - 0.999**3
clip_limit = 0.25 * math.sqrt(ND * NM * B * B)


def await_bytes(ref, sem):
    pltpu.make_async_copy(ref, ref, sem).wait()


def kernel(grad, owners, left, right, first, second, out,
           gbuf, lv, lt, rv, m1v, m2v, send2, tile, rot, turned, step, back, send3, send4, landed,
           inverse, part, part_z, part_x, part_m,
           s1s, s1r, s2s, s2r, s3s, s3r, s4s, s4r, pss, psr, loc, *arrivals):
    recv1, recv3 = arrivals[:C], arrivals[C:]
    d = lax.axis_index("dp")
    m = lax.axis_index("mp")
    z, x = d // NX, d % NX

    barrier = pltpu.get_barrier_semaphore()

    def greet(i, _):
        pl.semaphore_signal(barrier, inc=1, device_id=((d + i) % ND, m), device_id_type=MESH)
        return 0

    def greet_m(i, _):
        pl.semaphore_signal(barrier, inc=1, device_id=(d, (m + i) % NM), device_id_type=MESH)
        return 0

    local = [
        pltpu.make_async_copy(grad, gbuf, loc.at[0]),
        pltpu.make_async_copy(left.at[0], lv, loc.at[1]),
        pltpu.make_async_copy(right.at[0], rv, loc.at[2]),
        pltpu.make_async_copy(first.at[0], m1v, loc.at[3]),
        pltpu.make_async_copy(second.at[0], m2v, loc.at[4]),
    ]
    lax.fori_loop(1, ND, greet, 0)
    lax.fori_loop(1, NM, greet_m, 0)
    for copy in local:
        copy.start()
    pl.semaphore_wait(barrier, ND - 1 + NM - 1)

    def cols(k):
        return pl.ds(pl.multiple_of(k * W, W), W)

    def spread(k, i, _):
        to = (z + (i * 3) % NZ) % NZ
        pltpu.make_async_remote_copy(
            src_ref=grad.at[:, pl.ds(pl.multiple_of(to * H, H), H), cols(k)],
            dst_ref=recv1[k].at[pl.ds(z * S, S)],
            send_sem=s1s.at[k],
            recv_sem=s1r.at[k],
            device_id=(to * NX + x, m),
            device_id_type=MESH,
        ).start()
        return 0

    for k in range(C):
        lax.fori_loop(1, NZ, functools.partial(spread, k), 0)

    local[0].wait()

    def squares(i, acc):
        block = gbuf[i // 16, pl.ds(pl.multiple_of((i % 16) * 16, 16), 16), :].astype(jnp.float32)
        return acc + block * block

    acc = lax.fori_loop(0, 64, squares, jnp.zeros((16, B), jnp.float32))
    acc = acc[:8] + acc[8:]
    total = acc[:, :128]
    for i in range(1, 8):
        total = total + acc[:, i * 128 : (i + 1) * 128]
    part[0] = total
    part_z[z] = total

    def tell_z(i, _):
        to = (z + i) % NZ
        pltpu.make_async_remote_copy(
            src_ref=part.at[0], dst_ref=part_z.at[z], send_sem=pss.at[0], recv_sem=psr.at[0],
            device_id=(to * NX + x, m), device_id_type=MESH,
        ).start()
        return 0

    lax.fori_loop(1, NZ, tell_z, 0)

    def invert(o, _):
        found = jnp.int32(0)
        for j in range(ND):
            found = found + jnp.where(owners[j * NM + m] == o, (j % NZ) * S + j // NZ, 0)
        inverse[o] = jnp.minimum(found, ND - 1)
        return 0

    lax.fori_loop(0, ND, invert, 0)

    local[1].wait()

    def turn(i, _):
        rows = pl.ds(pl.multiple_of(i * T, T), T)
        lt[:, rows] = lv[rows, :].T
        return 0

    lax.fori_loop(0, B // T, turn, 0)

    def forward(k):
        for s in range(S):
            recv1[k][z * S + s] = gbuf[s, pl.ds(pl.multiple_of(z * H, H), H), cols(k)]
        await_bytes(recv1[k].at[pl.ds(0, 7 * S)], s1r.at[k])

        def send(i, _):
            o = ((z + ((i // NX) * 3) % NZ) % NZ) * NX + (x + i % NX) % NX
            send2[k, o] = recv1[k][inverse[o]]
            pltpu.make_async_remote_copy(
                src_ref=send2.at[k, o],
                dst_ref=tile.at[k, pl.ds(pl.multiple_of(x * Q + z * H, H), H), :],
                send_sem=s2s.at[k],
                recv_sem=s2r.at[k],
                device_id=(o, m),
                device_id_type=MESH,
            ).start()
            return 0

        lax.fori_loop(1, ND, send, 0)
        tile[k, pl.ds(pl.multiple_of(x * Q + z * H, H), H), :] = recv1[k][inverse[d]]

    for k in range(C):
        forward(k)

    await_bytes(part_z.at[pl.ds(0, 7)], psr.at[0])
    total = part_z[0]
    for i in range(1, NZ):
        total = total + part_z[i]
    part[1] = total
    part_x[x] = total

    def tell_x(i, _):
        pltpu.make_async_remote_copy(
            src_ref=part.at[1], dst_ref=part_x.at[x], send_sem=pss.at[1], recv_sem=psr.at[1],
            device_id=(z * NX + (x + i) % NX, m), device_id_type=MESH,
        ).start()
        return 0

    lax.fori_loop(1, NX, tell_x, 0)

    def clear(i, _):
        turned[pl.ds(pl.multiple_of(i * T, T), T), :] = jnp.zeros((T, B), jnp.float32)
        return 0

    lax.fori_loop(0, B // T, clear, 0)
    local[2].wait()

    def rotate(k, _):
        await_bytes(tile.at[k, pl.ds(0, 31 * H), :], s2r.at[k])

        def rows_of(i, _):
            rows = pl.ds(pl.multiple_of(i * T, T), T)
            rot[...] = jnp.dot(lt[rows, :], tile[k], preferred_element_type=jnp.float32).astype(jnp.bfloat16)
            turned[rows, :] += jnp.dot(rot[...], rv[cols(k), :], preferred_element_type=jnp.float32)
            return 0

        lax.fori_loop(0, B // T, rows_of, 0)
        return 0

    lax.fori_loop(0, 1, rotate, 0)
    await_bytes(part_x.at[pl.ds(0, 3)], psr.at[1])
    total = part_x[0]
    for i in range(1, NX):
        total = total + part_x[i]
    part[2] = total
    part_m[m] = total

    def tell_m(i, _):
        pltpu.make_async_remote_copy(
            src_ref=part.at[2], dst_ref=part_m.at[m], send_sem=pss.at[2], recv_sem=psr.at[2],
            device_id=(d, (m + i) % NM), device_id_type=MESH,
        ).start()
        return 0

    lax.fori_loop(1, NM, tell_m, 0)
    lax.fori_loop(1, C, rotate, 0)
    await_bytes(part_m.at[pl.ds(0, 7)], psr.at[2])
    total = part_m[0]
    for i in range(1, NM):
        total = total + part_m[i]
    total_squares = jnp.sum(total, keepdims=True)
    factor = jnp.minimum(jnp.float32(1.0), clip_limit / jnp.sqrt(total_squares))
    local[3].wait()
    local[4].wait()

    def precondition(i, _):
        rows = pl.ds(pl.multiple_of(i * 32, 32), 32)
        t = turned[rows, :] * factor
        first_new = beta_one * m1v[rows, :].astype(jnp.float32) + (1.0 - beta_one) * t
        second_new = beta_two * m2v[rows, :].astype(jnp.float32) + (1.0 - beta_two) * t * t
        value = first_new * (1.0 / correct_one) / (jnp.sqrt(second_new * (1.0 / correct_two)) + epsilon)
        step[rows, :] = value.astype(jnp.bfloat16)
        return 0

    lax.fori_loop(0, B // 32, precondition, 0)

    def produce(k):
        def columns_of(i, _):
            rows = pl.ds(pl.multiple_of(i * T, T), T)
            back[rows, :] = lax.dot_general(
                step[rows, :], rv[cols(k), :], (((1,), (1,)), ((), ())), preferred_element_type=jnp.float32
            ).astype(jnp.bfloat16)
            return 0

        lax.fori_loop(0, B // T, columns_of, 0)

        def rows_of(i, _):
            rows = pl.ds(pl.multiple_of(i * T, T), T)
            send3[k, rows, :] = jnp.dot(lv[rows, :], back[...], preferred_element_type=jnp.float32).astype(jnp.bfloat16)
            return 0

        lax.fori_loop(0, B // T, rows_of, 0)

        def send(i, _):
            zz, xx = (z + ((i // NX) * 3) % NZ) % NZ, (x + i % NX) % NX
            pltpu.make_async_remote_copy(
                src_ref=send3.at[k, pl.ds(pl.multiple_of(xx * Q + zz * H, H), H), :],
                dst_ref=recv3[k].at[d],
                send_sem=s3s.at[k],
                recv_sem=s3r.at[k],
                device_id=(zz * NX + xx, m),
                device_id_type=MESH,
            ).start()
            return 0

        lax.fori_loop(1, ND, send, 0)
        recv3[k][d] = send3[k, pl.ds(pl.multiple_of(x * Q + z * H, H), H), :]

    for k in range(C):
        produce(k)

    def collect(k):
        await_bytes(recv3[k].at[pl.ds(0, 31)], s3r.at[k])

        def send(i, _):
            to = (z + (i * 3) % NZ) % NZ
            for s in range(S):
                send4[k, to, s] = recv3[k][owners[(s * NZ + to) * NM + m]]
            pltpu.make_async_remote_copy(
                src_ref=send4.at[k, to],
                dst_ref=landed.at[:, pl.ds(pl.multiple_of(z * H, H), H), cols(k)],
                send_sem=s4s.at[k],
                recv_sem=s4r.at[k],
                device_id=(to * NX + x, m),
                device_id_type=MESH,
            ).start()
            return 0

        lax.fori_loop(1, NZ, send, 0)
        for s in range(S):
            landed[s, pl.ds(pl.multiple_of(z * H, H), H), cols(k)] = recv3[k][owners[(s * NZ + z) * NM + m]]

    for k in range(C):
        collect(k)

    def finish(k, _):
        await_bytes(send4.at[k, pl.ds(0, 7)], s4r.at[k])
        pltpu.make_async_copy(landed.at[:, :, cols(k)], out.at[:, :, cols(k)], loc.at[5]).start()
        return 0

    lax.fori_loop(0, C, finish, 0)

    def drain(k, _):
        await_bytes(send4.at[k, pl.ds(0, 7)], s1s.at[k])
        await_bytes(send2.at[k, pl.ds(0, 31)], s2s.at[k])
        await_bytes(send2.at[k, pl.ds(0, 31)], s3s.at[k])
        await_bytes(send4.at[k, pl.ds(0, 7)], s4s.at[k])
        return 0

    lax.fori_loop(0, C, drain, 0)
    await_bytes(part_z.at[pl.ds(0, 7)], pss.at[0])
    await_bytes(part_x.at[pl.ds(0, 3)], pss.at[1])
    await_bytes(part_m.at[pl.ds(0, 7)], pss.at[2])
    await_bytes(landed, loc.at[5])


def per_device(*args):
    bf16, f32 = jnp.bfloat16, jnp.float32
    whole = pl.BlockSpec(memory_space=pl.ANY)
    dma = pltpu.SemaphoreType.DMA
    return pl.pallas_call(
        kernel,
        out_shape=jax.ShapeDtypeStruct((S, Q, B), bf16),
        in_specs=[whole, pl.BlockSpec(memory_space=pltpu.SMEM), whole, whole, whole, whole],
        out_specs=whole,
        scratch_shapes=[
            pltpu.VMEM((S, Q, B), bf16),
            pltpu.VMEM((B, B), bf16),
            pltpu.VMEM((B, B), bf16),
            pltpu.VMEM((B, B), bf16),
            pltpu.VMEM((B, B), bf16),
            pltpu.VMEM((B, B), bf16),
            pltpu.VMEM((C, ND, H, W), bf16),
            pltpu.VMEM((C, B, W), bf16),
            pltpu.VMEM((T, W), bf16),
            pltpu.VMEM((B, B), f32),
            pltpu.VMEM((B, B), bf16),
            pltpu.VMEM((B, W), bf16),
            pltpu.VMEM((C, B, W), bf16),
            pltpu.VMEM((C, NZ, S, H, W), bf16),
            pltpu.VMEM((S, Q, B), bf16),
            pltpu.SMEM((ND,), jnp.int32),
            pltpu.VMEM((3, 8, 128), f32),
            pltpu.VMEM((NZ, 8, 128), f32),
            pltpu.VMEM((NX, 8, 128), f32),
            pltpu.VMEM((NM, 8, 128), f32),
        ]
        + [dma((C,))] * 8
        + [dma((3,)), dma((3,)), dma((6,))]
        + [pltpu.VMEM((ND, H, W), bf16)] * (2 * C),
        compiler_params=pltpu.CompilerParams(collective_id=0, has_side_effects=True, vmem_limit_bytes=56 << 20),
        cost_estimate=pl.CostEstimate(flops=8 * B**3, bytes_accessed=14 * B * B, transcendentals=2 * B * B),
        name="soap_step",
    )(*args)


def solution(mesh):
    placed = (
        P(None, "dp", "mp"),
        P(),
        P(("dp", "mp"), None, None),
        P(("dp", "mp"), None, None),
        P(("dp", "mp"), None, None),
        P(("dp", "mp"), None, None),
    )
    return jax.shard_map(
        per_device, mesh=mesh, in_specs=placed, out_specs=P(None, "dp", "mp"), check_vma=False
    )
```

time: 337 us -> 210 us (0.62)
  Pallas kernels: 0 us -> 207 us
  blocking collectives: 143 us -> 0 us
  waiting for transfers between devices: 98.7 us -> 0 us
  local copies, waits for them, and re-layouts: 34.6 us -> 3.08 us
  starting transfers between devices: 25.4 us -> 0 us
  matrix products: 23.2 us -> 0 us
  other arithmetic: 8.75 us -> 0 us
    pallas_call x0 -> x1, Pallas kernels: none -> 207 us  [per_device(): pl.pallas_call(kernel, out_shape=jax.ShapeDtypeStruct((S, Q, B), bf16), i...]
    all_to_all x3 -> x0, waiting for transfers between devices: 98.7 us -> none  [the longest x1 49.6 us: per_device(): lax.all_to_all(result.reshape(block_size, data_size, width), 'dp', split_...]
    psum x1 -> x0, blocking collectives: 87.8 us -> none  [per_device(): total_squares = lax.psum(local_squares, ('dp', 'mp'))]
    all_to_all x1 -> x0, blocking collectives: 55 us -> none  [per_device(): lax.all_to_all(spread_out, 'dp', split_axis=0, concat_axis=3, tiled=True)]
    all_to_all x3 -> x0, starting transfers between devices: 25.4 us -> none  [the longest x1 11.6 us: per_device(): lax.all_to_all(pieces, 'dp', split_axis=2, concat_axis=0, tiled=True)]
    dot_general x3 -> x0, matrix products: 23.2 us -> none  [the longest x1 12.7 us: per_device(): lax.dot_general(step_rotated, right_tile, (((1,), (1,)), ((), ())), prefe...]
    reshape x5 -> x0, local copies, waits for them, and re-layouts: 16.5 us -> none  [the longest x1 4.87 us: per_device(): arrived.reshape(groups, quarters, quarters, row_part, width)]
    gather x3 -> x0, local copies, waits for them, and re-layouts: 11.7 us -> none  [the longest x2 8.09 us: per_device(): by_tile = jnp.take(back, column_owners, axis=1)]
  transfers between devices with their start and end apart: 3 -> 0, of which waited for: 2 -> 0; matrix products, arithmetic and copies ran while one was open for 1% -> 0% of each run, Pallas kernels for 0% -> 0%
where the time goes in v1:
time: 210 us
  Pallas kernels  207 us (99%)
  local copies, waits for them, and re-layouts  3.08 us (1%)
    pallas_call x1, Pallas kernels, per_device(): pl.pallas_call(kernel, out_shape=jax.ShapeDtypeStruct((S, Q, B), bf16), i...  207 us

profile of v1, /device:TPU:8, one launch (start us, length us, event | category | flops | bytes accessed | tf_op | source)
XLA Modules:
  0.0 209.9 jit_solution(13492003104032918130)
XLA Ops:
  0.0 206.8 %soap_step.1 = bf16[4,256,1024]{2,1,0:T(8,128)(2,1)} custom-call(bf16[4,256,1024]{2,1,0:T(8,128)(2,1)} %grad.1, s32[256]{0:T(256)} %owners.1, bf16[1,1024,1024]{2,1,0:T(8,128)(2,1)} %left.1, bf16[1,1024,1024]{2,1,0:T(8,128)(2,1)} %right.1, bf16[1,1024,1024]{2,1,0:T(8,128)(2,1)} %first.1, bf16[1,1024,1024]{2,1,0:T(8,128)(2,1)} %second.1), custom_call_target="tpu_custom_call" | custom-call | flops 8589934592 | bytes 14680064 | tf_op jit(solution)/shard_map/soap_step/pallas_call | solution.py:306
  206.8 3.1 %copy.8 = bf16[4,256,1024]{2,1,0:T(8,128)(2,1)} copy(bf16[4,256,1024]{2,1,0:T(8,128)(2,1)} %soap_step.1) | data formatting | bytes 4194304

commit v2 on v0

v2 whole, which is shorter than its diff:
```python
import math

import jax
import jax.numpy as jnp
from jax import lax
from jax.experimental import pallas as pl
from jax.experimental.pallas import tpu as pltpu
from jax.sharding import PartitionSpec as P

MESH = pl.DeviceIdType.MESH
B = 1024
S = 4
NZ, NX, NM = 8, 4, 8
ND = NZ * NX
Q = B // NX
H = Q // NZ
C = 4
W = B // C
T = 256
R = NX * H

beta_one = 0.9
beta_two = 0.999
epsilon = 1e-08
correct_one = 1.0 - 0.9**3
correct_two = 1.0 - 0.999**3
clip_limit = 0.25 * math.sqrt(ND * NM * B * B)


def await_bytes(ref, sem):
    pltpu.make_async_copy(ref, ref, sem).wait()


def send(src, dst, send_sem, recv_sem, to):
    pltpu.make_async_remote_copy(
        src_ref=src, dst_ref=dst, send_sem=send_sem, recv_sem=recv_sem, device_id=to, device_id_type=MESH
    ).start()


class Ring:
    def __init__(self, source, deliver, spread, refs):
        self.source, self.deliver, self.spread = source, deliver, spread
        self.t1, self.t2, self.t3, self.ss, self.st, self.sf = refs
        d, self.m = lax.axis_index("dp"), lax.axis_index("mp")
        self.z, self.x = d // NX, d % NX

    def ways(self):
        for i, way in ((0, 1), (1, NZ - 1)):
            yield i, way, (((self.z + way) % NZ) * NX + self.x, self.m)

    def off(self, n):
        return (self.z + n) % NZ

    def land(self, piece, k, origin, way, hop, part):
        sem = self.sf.at[hop if self.spread == "hop" else k]
        zz = self.off(way)
        if not self.spread:
            send(piece(part), self.deliver(k, origin, part), self.ss.at[3, k], sem, (zz * NX + self.x, self.m))
            return
        for n in range(part.size):
            j = part.start + (self.x + n) % part.size
            send(piece(pl.ds(j, 1)), self.deliver(k, origin), self.ss.at[3, k], sem, (zz * NX + j, self.m))

    def hop1(self, k, planes=(4, 3, 2, 1)):
        for i, way, to in self.ways():
            for n, place in ((4, pl.ds(0, 2)), (3, pl.ds(2, 4)), (2, pl.ds(6, 4))):
                if n in planes:
                    zz, part = (self.off(4), pl.ds(2 * i, 2)) if n == 4 else (self.off(n * way), ALL)
                    send(self.source(k, zz, part), self.t1.at[i, k, place], self.ss.at[0, k], self.st.at[i, 0, k], to)
            if 1 in planes:
                self.land(lambda p: self.source(k, self.off(way), p), k, self.z, way, 1, ALL)

    def hop2(self, k):
        for i, way, to in self.ways():
            await_bytes(self.t1.at[i, k], self.st.at[i, 0, k])
            send(self.t1.at[i, k, pl.ds(0, 6)], self.t2.at[i, k], self.ss.at[1, k], self.st.at[i, 1, k], to)
            self.land(lambda p: self.t1.at[i, k, pl.ds(6 + p.start, p.size)], k, self.off(NZ - way), way, 2, ALL)

    def hop3(self, k):
        for i, way, to in self.ways():
            await_bytes(self.t2.at[i, k], self.st.at[i, 1, k])
            send(self.t2.at[i, k, pl.ds(0, 2)], self.t3.at[i, k], self.ss.at[2, k], self.st.at[i, 2, k], to)
            self.land(lambda p: self.t2.at[i, k, pl.ds(2 + p.start, p.size)], k, self.off(2 * (NZ - way)), way, 3, ALL)

    def hop4(self, k):
        for i, way, to in self.ways():
            await_bytes(self.t3.at[i, k], self.st.at[i, 2, k])
            self.land(
                lambda p: self.t3.at[i, k, pl.ds(p.start - 2 * i, p.size)],
                k, self.off(3 * (NZ - way)), way, 4, pl.ds(2 * i, 2))

    def along_x(self, k):
        for i in range(1, NX):
            xx = (self.x + i) % NX
            send(self.source(k, self.z, pl.ds(xx, 1)), self.deliver(k, self.z), self.ss.at[3, k],
                 self.sf.at[0 if self.spread == "hop" else k], (self.z * NX + xx, self.m))

    def drain(self, k, whole):
        await_bytes(self.t1.at[:, k], self.ss.at[0, k])
        await_bytes(self.t2.at[:, k], self.ss.at[1, k])
        await_bytes(self.t3.at[:, k], self.ss.at[2, k])
        await_bytes(whole.at[pl.ds(0, 31 if self.spread else 28)], self.ss.at[3, k])


ALL = pl.ds(0, 4)


def cols(k):
    return pl.ds(k * W, W)


def rows_of_plane(zz):
    return pl.ds(pl.multiple_of(zz * H, H), H)


def kernel(grad, owners, left, right, first, second, out,
           gbuf, lv, lt, rv, m1v, m2v, send2, tile, half, turned, step, send3, send4,
           inverse, part, part_z, part_x, part_m, pss, psr, loc, *more):
    recv1, recv3, more = more[:C], more[C : 2 * C], more[2 * C :]
    d = lax.axis_index("dp")
    m = lax.axis_index("mp")
    z, x = d // NX, d % NX

    ring1 = Ring(
        lambda k, zz, part: gbuf.at[part, rows_of_plane(zz), cols(k)],
        lambda k, zz, part: recv1[k].at[pl.ds(zz * S + part.start, part.size)],
        None, more[0:6])
    ring2 = Ring(
        lambda k, zz, part: send2.at[k, pl.ds(zz * NX + part.start, part.size)],
        lambda k, zz: tile.at[zz, pl.ds(x, 1), :, cols(k)],
        "hop", more[6:12])
    ring3 = Ring(
        lambda k, zz, part: send3.at[zz, part, :, cols(k)],
        lambda k, zz: recv3[k].at[pl.ds(zz * NX + x, 1)],
        "chunk", more[12:18])
    ring4 = Ring(
        lambda k, zz, part: send4.at[k, zz, part],
        lambda k, zz, part: out.at[part, rows_of_plane(zz), cols(k)],
        None, more[18:24])

    barrier = pltpu.get_barrier_semaphore()

    def along_z(i):
        return (((z + i) % NZ) * NX + x, m)

    def along_x(i):
        return (z * NX + (x + i) % NX, m)

    def along_m(i):
        return (d, (m + i) % NM)

    local = [
        pltpu.make_async_copy(grad, gbuf, loc.at[0]),
        pltpu.make_async_copy(right.at[0], rv, loc.at[2]),
        pltpu.make_async_copy(first.at[0], m1v, loc.at[3]),
        pltpu.make_async_copy(second.at[0], m2v, loc.at[4]),
    ]
    local[0].start()

    met = [along_z(i) for i in range(1, NZ)] + [along_x(i) for i in range(1, NX)] + [along_m(i) for i in range(1, NM)]
    met += [(((z + way) % NZ) * NX + (x + i) % NX, m) for way in (1, NZ - 1) for i in range(1, NX)]
    for other in met:
        pl.semaphore_signal(barrier, inc=1, device_id=other, device_id_type=MESH)
    local[0].wait()
    pl.semaphore_wait(barrier, len(met))

    def gather_sum(n, value, held, place, axis, size):
        part[n] = value
        held[place] = value
        for i in range(1, size):
            send(part.at[n], held.at[place], pss.at[n], psr.at[n], axis(i))

    def sum_of(n, held, size):
        await_bytes(held.at[pl.ds(0, size - 1)], psr.at[n])
        total = held[0]
        for i in range(1, size):
            total = total + held[i]
        return total

    def squares():
        def add(i, acc):
            block = gbuf[i // 16, pl.ds(pl.multiple_of((i % 16) * 16, 16), 16), :].astype(jnp.float32)
            return acc + block * block

        acc = lax.fori_loop(0, 64, add, jnp.zeros((16, B), jnp.float32))
        acc = acc[:8] + acc[8:]
        total = acc[:, :128]
        for i in range(1, 8):
            total = total + acc[:, i * 128 : (i + 1) * 128]
        gather_sum(0, total, part_z, z, along_z, NZ)

    def invert(low, high):
        def one(o, _):
            found = jnp.int32(0)
            for j in range(ND):
                found = found + jnp.where(owners[j * NM + m] == o, (j % NZ) * S + j // NZ, 0)
            inverse[o] = jnp.minimum(found, ND - 1)
            return 0

        lax.fori_loop(low, high, one, 0)

    def fetch():
        def one(i, _):
            rows = pl.ds(pl.multiple_of((i % NX) * Q + (i // NX) * H, H), H)
            pltpu.make_async_copy(left.at[0, rows, :], lv.at[i // NX, i % NX], loc.at[1]).start()
            return 0

        lax.fori_loop(0, ND, one, 0)
        for copy in local[1:]:
            copy.start()

    def lanes(zz):
        return pl.ds(pl.multiple_of(zz * R, R), R)

    def turn():
        await_bytes(lv, loc.at[1])

        def one(zz, _):
            lt[:, lanes(zz)] = lv[zz].reshape(R, B).T
            turned[lanes(zz), :] = jnp.zeros((R, B), jnp.float32)
            return 0

        lax.fori_loop(0, NZ, one, 0)

    def pack(k):
        for s in range(S):
            recv1[k][z * S + s] = gbuf[s, rows_of_plane(z), cols(k)]
        await_bytes(recv1[k].at[pl.ds(0, 28)], ring1.sf.at[k])

        def one(o, _):
            send2[k, o] = recv1[k][inverse[o]]
            return 0

        lax.fori_loop(0, ND, one, 0, unroll=4)

    def rows_by(ref, planes):
        return jnp.concatenate([ref[zz].reshape(R, B) for zz in planes], axis=0)

    def rotate(*shifts):
        planes = [(z + n) % NZ for n in shifts]
        size = R * len(planes)

        def columns_of(i, _):
            wide = pl.ds(pl.multiple_of(i * T, T), T)
            half[:size, wide] = jnp.dot(
                rows_by(tile, planes), rv[:, wide], preferred_element_type=jnp.float32
            ).astype(jnp.bfloat16)
            return 0

        lax.fori_loop(0, B // T, columns_of, 0)

        def rows_of(i, _):
            rows = pl.ds(pl.multiple_of(i * T, T), T)
            basis = jnp.concatenate([lt[rows, lanes(zz)] for zz in planes], axis=1)
            turned[rows, :] += jnp.dot(basis, half[:size], preferred_element_type=jnp.float32)
            return 0

        lax.fori_loop(0, B // T, rows_of, 0)

    for k in range(C):
        ring1.hop1(k)
    squares()
    fetch()

    def onward(k):
        pack(k)
        ring2.hop1(k)
        ring2.along_x(k)
        tile[z, pl.ds(x, 1), :, cols(k)] = send2[k, pl.ds(d, 1)]

    early, late = range(C // 2), range(C // 2, C)

    def run(*steps):
        for step_of, chunks in steps:
            for k in chunks:
                step_of(k)

    run((ring1.hop2, early))
    invert(0, ND // 2)
    run((ring1.hop3, early), (ring1.hop2, late))
    invert(ND // 2, ND)
    turn()
    run((ring1.hop4, early), (ring1.hop3, late), (onward, early), (ring1.hop4, late), (onward, late))
    gather_sum(1, sum_of(0, part_z, NZ), part_x, x, along_x, NX)
    for k in range(C):
        ring2.hop2(k)
    local[1].wait()
    await_bytes(tile.at[0, pl.ds(0, NX - 1)], ring2.sf.at[0])
    rotate(0)
    gather_sum(2, sum_of(1, part_x, NX), part_m, m, along_m, NM)
    for k in range(C):
        ring2.hop3(k)
    await_bytes(tile.at[pl.ds(0, 2)], ring2.sf.at[1])
    rotate(1, 7)
    for k in range(C):
        ring2.hop4(k)
    await_bytes(tile.at[pl.ds(0, 2)], ring2.sf.at[2])
    rotate(2, 6)
    await_bytes(tile.at[pl.ds(0, 2)], ring2.sf.at[3])
    rotate(3, 5)
    await_bytes(tile.at[0], ring2.sf.at[4])
    rotate(4)

    total_squares = jnp.sum(sum_of(2, part_m, NM), keepdims=True)
    factor = jnp.minimum(jnp.float32(1.0), clip_limit / jnp.sqrt(total_squares))
    local[2].wait()
    local[3].wait()

    def precondition(i, _):
        rows = pl.ds(pl.multiple_of(i * 32, 32), 32)
        t = turned[rows, :] * factor
        first_new = (beta_one / correct_one) * m1v[rows, :].astype(jnp.float32) + ((1.0 - beta_one) / correct_one) * t
        second_new = (beta_two / correct_two) * m2v[rows, :].astype(jnp.float32)
        second_new = second_new + ((1.0 - beta_two) / correct_two) * (t * t)
        value = first_new / (second_new * lax.rsqrt(second_new) + epsilon)
        step[rows, :] = value.astype(jnp.bfloat16)
        return 0

    lax.fori_loop(0, B // 32, precondition, 0)

    def produce(*shifts):
        planes = [(z + n) % NZ for n in shifts]
        size = R * len(planes)

        def columns_of(i, _):
            wide = pl.ds(pl.multiple_of(i * T, T), T)
            half[:size, wide] = jnp.dot(
                rows_by(lv, planes), step[:, wide], preferred_element_type=jnp.float32
            ).astype(jnp.bfloat16)
            return 0

        lax.fori_loop(0, B // T, columns_of, 0)

        def back(i, _):
            wide = pl.ds(pl.multiple_of(i * T, T), T)
            value = lax.dot_general(
                half[:size], rv[wide, :], (((1,), (1,)), ((), ())), preferred_element_type=jnp.float32
            ).astype(jnp.bfloat16)
            for n, zz in enumerate(planes):
                send3[zz, :, :, wide] = value[n * R : (n + 1) * R].reshape(NX, H, T)
            return 0

        lax.fori_loop(0, B // T, back, 0)

    for n in (4, 3, 2, 1):
        produce(*sorted({n, NZ - n}))
        for k in range(C):
            ring3.hop1(k, (n,))
    produce(0)
    for k in range(C):
        ring3.along_x(k)
        recv3[k][pl.ds(d, 1)] = send3[z, pl.ds(x, 1), :, cols(k)]

    def place(k):
        await_bytes(recv3[k].at[pl.ds(0, 31)], ring3.sf.at[k])

        def one(zz, _):
            for s in range(S):
                send4[k, zz, s] = recv3[k][owners[(s * NZ + zz) * NM + m]]
            return 0

        lax.fori_loop(0, NZ, one, 0)
        ring4.hop1(k)
        out[:, rows_of_plane(z), cols(k)] = send4[k, z]

    def finish(k):
        await_bytes(send4.at[k, pl.ds(0, 7)], ring4.sf.at[k])

    run((ring3.hop2, early), (ring3.hop3, early), (ring3.hop2, late), (ring3.hop4, early), (ring3.hop3, late))
    run((place, early), (ring3.hop4, late), (place, late))
    run((ring4.hop2, range(C)), (ring4.hop3, range(C)), (ring4.hop4, range(C)), (finish, range(C)))

    for k in range(C):
        for ring in (ring1, ring2, ring3, ring4):
            ring.drain(k, recv1[k])
    await_bytes(part_z.at[pl.ds(0, NZ - 1)], pss.at[0])
    await_bytes(part_x.at[pl.ds(0, NX - 1)], pss.at[1])
    await_bytes(part_m.at[pl.ds(0, NM - 1)], pss.at[2])


def per_device(*args):
    bf16, f32 = jnp.bfloat16, jnp.float32
    whole = pl.BlockSpec(memory_space=pl.ANY)
    dma = pltpu.SemaphoreType.DMA

    def vmem(*shape):
        return pltpu.VMEM(shape, bf16)

    ring = [vmem(2, C, 10, H, W), vmem(2, C, 6, H, W), vmem(2, C, 2, H, W), dma((4, C)), dma((2, 3, C)), dma((max(C, 5),))]
    return pl.pallas_call(
        kernel,
        out_shape=vmem(S, Q, B),
        in_specs=[whole, pl.BlockSpec(memory_space=pltpu.SMEM), whole, whole, whole, whole],
        out_specs=pl.BlockSpec(memory_space=pltpu.VMEM),
        scratch_shapes=[
            vmem(S, Q, B),
            vmem(NZ, NX, H, B),
            vmem(B, B),
            vmem(B, B),
            vmem(B, B),
            vmem(B, B),
            vmem(C, ND, H, W),
            vmem(NZ, NX, H, B),
            vmem(2 * R, B),
            pltpu.VMEM((B, B), f32),
            vmem(B, B),
            vmem(NZ, NX, H, B),
            vmem(C, NZ, S, H, W),
            pltpu.SMEM((ND,), jnp.int32),
            pltpu.VMEM((3, 8, 128), f32),
            pltpu.VMEM((NZ, 8, 128), f32),
            pltpu.VMEM((NX, 8, 128), f32),
            pltpu.VMEM((NM, 8, 128), f32),
            dma((3,)),
            dma((3,)),
            dma((6,)),
        ]
        + [vmem(ND, H, W)] * (2 * C)
        + ring * 4,
        compiler_params=pltpu.CompilerParams(collective_id=0, has_side_effects=True, vmem_limit_bytes=58 << 20),
        cost_estimate=pl.CostEstimate(flops=8 * B**3, bytes_accessed=14 * B * B, transcendentals=2 * B * B),
        name="soap_step",
    )(*args)


def solution(mesh):
    placed = (
        P(None, "dp", "mp"),
        P(),
        P(("dp", "mp"), None, None),
        P(("dp", "mp"), None, None),
        P(("dp", "mp"), None, None),
        P(("dp", "mp"), None, None),
    )
    return jax.shard_map(
        per_device, mesh=mesh, in_specs=placed, out_specs=P(None, "dp", "mp"), check_vma=False
    )
```

time: 337 us -> 208 us (0.62)
  Pallas kernels: 0 us -> 206 us
  blocking collectives: 143 us -> 0 us
  waiting for transfers between devices: 98.7 us -> 0 us
  local copies, waits for them, and re-layouts: 34.6 us -> 1.32 us
  starting transfers between devices: 25.4 us -> 0 us
  matrix products: 23.2 us -> 0 us
  other arithmetic: 8.75 us -> 0 us
    pallas_call x0 -> x1, Pallas kernels: none -> 206 us  [per_device(): pl.pallas_call(kernel, out_shape=vmem(S, Q, B), in_specs=[whole, pl.Block...]
    all_to_all x3 -> x0, waiting for transfers between devices: 98.7 us -> none  [the longest x1 49.6 us: per_device(): lax.all_to_all(result.reshape(block_size, data_size, width), 'dp', split_...]
    psum x1 -> x0, blocking collectives: 87.8 us -> none  [per_device(): total_squares = lax.psum(local_squares, ('dp', 'mp'))]
    all_to_all x1 -> x0, blocking collectives: 55 us -> none  [per_device(): lax.all_to_all(spread_out, 'dp', split_axis=0, concat_axis=3, tiled=True)]
    all_to_all x3 -> x0, starting transfers between devices: 25.4 us -> none  [the longest x1 11.6 us: per_device(): lax.all_to_all(pieces, 'dp', split_axis=2, concat_axis=0, tiled=True)]
    dot_general x3 -> x0, matrix products: 23.2 us -> none  [the longest x1 12.7 us: per_device(): lax.dot_general(step_rotated, right_tile, (((1,), (1,)), ((), ())), prefe...]
    reshape x5 -> x0, local copies, waits for them, and re-layouts: 16.5 us -> none  [the longest x1 4.87 us: per_device(): arrived.reshape(groups, quarters, quarters, row_part, width)]
    gather x3 -> x0, local copies, waits for them, and re-layouts: 11.7 us -> none  [the longest x2 8.09 us: per_device(): by_tile = jnp.take(back, column_owners, axis=1)]
  transfers between devices with their start and end apart: 3 -> 0, of which waited for: 2 -> 0; matrix products, arithmetic and copies ran while one was open for 1% -> 0% of each run, Pallas kernels for 0% -> 0%
where the time goes in v2:
time: 208 us
  Pallas kernels  206 us (99%)
    pallas_call x1, Pallas kernels, per_device(): pl.pallas_call(kernel, out_shape=vmem(S, Q, B), in_specs=[whole, pl.Block...  206 us

profile of v2, /device:TPU:8, one launch (start us, length us, event | category | flops | bytes accessed | tf_op | source)
XLA Modules:
  0.0 207.5 jit_solution(8028454327944017263)
XLA Ops:
  0.0 206.2 %soap_step.1 = bf16[4,256,1024]{2,1,0:T(8,128)(2,1)S(1)} custom-call(bf16[4,256,1024]{2,1,0:T(8,128)(2,1)} %grad.1, s32[256]{0:T(256)} %owners.1, bf16[1,1024,1024]{2,1,0:T(8,128)(2,1)} %left.1, bf16[1,1024,1024]{2,1,0:T(8,128)(2,1)} %right.1, bf16[1,1024,1024]{2,1,0:T(8,128)(2,1)} %first.1, bf16[1,1024,1024]{2,1,0:T(8,128)(2,1)} %second.1), custom_call_target="tpu_custom_call" | custom-call | flops 8589934592 | bytes 14680064 | tf_op jit(solution)/shard_map/soap_step/pallas_call | solution.py:390
  206.2 1.3 copy.8

commit v3 on v2

--- a/solution.py
+++ b/solution.py
@@ -17,6 +17,7 @@
 C = 4
 W = B // C
 T = 256
+E = 16
 R = NX * H
 
 beta_one = 0.9
@@ -114,9 +115,10 @@
 
 
 def kernel(grad, owners, left, right, first, second, out,
-           gbuf, lv, lt, rv, m1v, m2v, send2, tile, half, turned, step, send3, send4,
+           gbuf, lv, lt, rv, rt, m1v, m2v, send2, tile, half, rest0, rest1, turned, step, send3, send4,
            inverse, part, part_z, part_x, part_m, pss, psr, loc, *more):
     recv1, recv3, more = more[:C], more[C : 2 * C], more[2 * C :]
+    rest = (rest0, rest1)
     d = lax.axis_index("dp")
     m = lax.axis_index("mp")
     z, x = d // NX, d % NX
@@ -217,7 +219,6 @@
 
         def one(zz, _):
             lt[:, lanes(zz)] = lv[zz].reshape(R, B).T
-            turned[lanes(zz), :] = jnp.zeros((R, B), jnp.float32)
             return 0
 
         lax.fori_loop(0, NZ, one, 0)
@@ -236,23 +237,32 @@
     def rows_by(ref, planes):
         return jnp.concatenate([ref[zz].reshape(R, B) for zz in planes], axis=0)
 
-    def rotate(*shifts):
+    def rotate_rows(at, *shifts):
         planes = [(z + n) % NZ for n in shifts]
         size = R * len(planes)
 
         def columns_of(i, _):
             wide = pl.ds(pl.multiple_of(i * T, T), T)
-            half[:size, wide] = jnp.dot(
+            half[at : at + size, wide] = jnp.dot(
                 rows_by(tile, planes), rv[:, wide], preferred_element_type=jnp.float32
             ).astype(jnp.bfloat16)
             return 0
 
         lax.fori_loop(0, B // T, columns_of, 0)
 
+    def left_rows(rows, *shifts):
+        basis = jnp.concatenate([lt[rows, lanes((z + n) % NZ)] for n in shifts], axis=1)
+        return jnp.dot(basis, half[: R * len(shifts)], preferred_element_type=jnp.float32)
+
+    def rotate(*shifts):
+        rotate_rows(0, *shifts)
+
         def rows_of(i, _):
             rows = pl.ds(pl.multiple_of(i * T, T), T)
-            basis = jnp.concatenate([lt[rows, lanes(zz)] for zz in planes], axis=1)
-            turned[rows, :] += jnp.dot(basis, half[:size], preferred_element_type=jnp.float32)
+            if shifts == (0,):
+                turned[rows, :] = left_rows(rows, *shifts)
+            else:
+                turned[rows, :] += left_rows(rows, *shifts)
             return 0
 
         lax.fori_loop(0, B // T, rows_of, 0)
@@ -268,25 +278,31 @@
         ring2.along_x(k)
         tile[z, pl.ds(x, 1), :, cols(k)] = send2[k, pl.ds(d, 1)]
 
-    early, late = range(C // 2), range(C // 2, C)
-
     def run(*steps):
-        for step_of, chunks in steps:
-            for k in chunks:
-                step_of(k)
-
-    run((ring1.hop2, early))
+        for step_of, k in steps:
+            step_of(k)
+
+    ring1.hop2(0)
     invert(0, ND // 2)
-    run((ring1.hop3, early), (ring1.hop2, late))
+    run((ring1.hop3, 0), (ring1.hop2, 1))
     invert(ND // 2, ND)
+    run((ring1.hop4, 0), (ring1.hop3, 1), (ring1.hop2, 2))
     turn()
-    run((ring1.hop4, early), (ring1.hop3, late), (onward, early), (ring1.hop4, late), (onward, late))
+    run((onward, 0), (ring1.hop4, 1), (ring1.hop3, 2), (ring1.hop2, 3))
+    run((onward, 1), (ring1.hop4, 2), (ring1.hop3, 3), (onward, 2), (ring1.hop4, 3), (onward, 3))
     gather_sum(1, sum_of(0, part_z, NZ), part_x, x, along_x, NX)
     for k in range(C):
         ring2.hop2(k)
     local[1].wait()
     await_bytes(tile.at[0, pl.ds(0, NX - 1)], ring2.sf.at[0])
     rotate(0)
+
+    def turn_right(i, _):
+        rows = pl.ds(pl.multiple_of(i * T, T), T)
+        rt[:, rows] = rv[rows, :].T
+        return 0
+
+    lax.fori_loop(0, B // T, turn_right, 0)
     gather_sum(2, sum_of(1, part_x, NX), part_m, m, along_m, NM)
     for k in range(C):
         ring2.hop3(k)
@@ -297,26 +313,30 @@
     await_bytes(tile.at[pl.ds(0, 2)], ring2.sf.at[2])
     rotate(2, 6)
     await_bytes(tile.at[pl.ds(0, 2)], ring2.sf.at[3])
-    rotate(3, 5)
+    rotate_rows(0, 3, 5)
     await_bytes(tile.at[0], ring2.sf.at[4])
-    rotate(4)
+    rotate_rows(2 * R, 4)
 
     total_squares = jnp.sum(sum_of(2, part_m, NM), keepdims=True)
     factor = jnp.minimum(jnp.float32(1.0), clip_limit / jnp.sqrt(total_squares))
     local[2].wait()
     local[3].wait()
 
-    def precondition(i, _):
-        rows = pl.ds(pl.multiple_of(i * 32, 32), 32)
-        t = turned[rows, :] * factor
-        first_new = (beta_one / correct_one) * m1v[rows, :].astype(jnp.float32) + ((1.0 - beta_one) / correct_one) * t
-        second_new = (beta_two / correct_two) * m2v[rows, :].astype(jnp.float32)
-        second_new = second_new + ((1.0 - beta_two) / correct_two) * (t * t)
-        value = first_new / (second_new * lax.rsqrt(second_new) + epsilon)
-        step[rows, :] = value.astype(jnp.bfloat16)
-        return 0
-
-    lax.fori_loop(0, B // 32, precondition, 0)
+    def precondition(i):
+        more = rest[i % 2]
+        more[...] = left_rows(pl.ds(i * T, T), 3, 5, 4)
+        for n in range(0, T, E):
+            rows = pl.ds(i * T + n, E)
+            t = (turned[rows, :] + more[n : n + E, :]) * factor
+            first_new = (beta_one / correct_one) * m1v[rows, :].astype(jnp.float32)
+            first_new = first_new + ((1.0 - beta_one) / correct_one) * t
+            second_new = (beta_two / correct_two) * m2v[rows, :].astype(jnp.float32)
+            second_new = second_new + ((1.0 - beta_two) / correct_two) * (t * t)
+            value = first_new / (second_new * lax.rsqrt(second_new) + epsilon)
+            step[rows, :] = value.astype(jnp.bfloat16)
+
+    for i in range(B // T):
+        precondition(i)
 
     def produce(*shifts):
         planes = [(z + n) % NZ for n in shifts]
@@ -333,9 +353,7 @@
 
         def back(i, _):
             wide = pl.ds(pl.multiple_of(i * T, T), T)
-            value = lax.dot_general(
-                half[:size], rv[wide, :], (((1,), (1,)), ((), ())), preferred_element_type=jnp.float32
-            ).astype(jnp.bfloat16)
+            value = jnp.dot(half[:size], rt[:, wide], preferred_element_type=jnp.float32).astype(jnp.bfloat16)
             for n, zz in enumerate(planes):
                 send3[zz, :, :, wide] = value[n * R : (n + 1) * R].reshape(NX, H, T)
             return 0
@@ -366,9 +384,12 @@
     def finish(k):
         await_bytes(send4.at[k, pl.ds(0, 7)], ring4.sf.at[k])
 
-    run((ring3.hop2, early), (ring3.hop3, early), (ring3.hop2, late), (ring3.hop4, early), (ring3.hop3, late))
-    run((place, early), (ring3.hop4, late), (place, late))
-    run((ring4.hop2, range(C)), (ring4.hop3, range(C)), (ring4.hop4, range(C)), (finish, range(C)))
+    run((ring3.hop2, 0), (ring3.hop3, 0), (ring3.hop2, 1), (ring3.hop4, 0), (ring3.hop3, 1), (ring3.hop2, 2))
+    run((place, 0), (ring3.hop4, 1), (ring3.hop3, 2), (ring3.hop2, 3), (place, 1), (ring3.hop4, 2), (ring3.hop3, 3))
+    run((place, 2), (ring3.hop4, 3), (place, 3))
+    for step_of in (ring4.hop2, ring4.hop3, ring4.hop4, finish):
+        for k in range(C):
+            step_of(k)
 
     for k in range(C):
         for ring in (ring1, ring2, ring3, ring4):
@@ -399,9 +420,12 @@
             vmem(B, B),
             vmem(B, B),
             vmem(B, B),
+            vmem(B, B),
             vmem(C, ND, H, W),
             vmem(NZ, NX, H, B),
-            vmem(2 * R, B),
+            vmem(3 * R, B),
+            pltpu.VMEM((T, B), f32),
+            pltpu.VMEM((T, B), f32),
             pltpu.VMEM((B, B), f32),
             vmem(B, B),
             vmem(NZ, NX, H, B),

time: 208 us -> 206 us (level)
    pallas_call x1, Pallas kernels: 206 us -> 204 us  [per_device(): pl.pallas_call(kernel, out_shape=vmem(S, Q, B), in_specs=[whole, pl.Block...]
where the time goes in v3:
time: 206 us; the launch traced here: 205 us
  Pallas kernels  204 us (99%)
    pallas_call x1, Pallas kernels, per_device(): pl.pallas_call(kernel, out_shape=vmem(S, Q, B), in_specs=[whole, pl.Block...  204 us

profile of v3, /device:TPU:8, one launch (start us, length us, event | category | flops | bytes accessed | tf_op | source)
XLA Modules:
  0.0 205.3 jit_solution(12930253417019863605)
XLA Ops:
  0.0 204.0 %soap_step.1 = bf16[4,256,1024]{2,1,0:T(8,128)(2,1)S(1)} custom-call(bf16[4,256,1024]{2,1,0:T(8,128)(2,1)} %grad.1, s32[256]{0:T(256)} %owners.1, bf16[1,1024,1024]{2,1,0:T(8,128)(2,1)} %left.1, bf16[1,1024,1024]{2,1,0:T(8,128)(2,1)} %right.1, bf16[1,1024,1024]{2,1,0:T(8,128)(2,1)} %first.1, bf16[1,1024,1024]{2,1,0:T(8,128)(2,1)} %second.1), custom_call_target="tpu_custom_call" | custom-call | flops 8589934592 | bytes 14680064 | tf_op jit(solution)/shard_map/soap_step/pallas_call | solution.py:411
  204.0 1.3 copy.8

commit v4 on v3

--- a/solution.py
+++ b/solution.py
@@ -62,8 +62,10 @@
             j = part.start + (self.x + n) % part.size
             send(piece(pl.ds(j, 1)), self.deliver(k, origin), self.ss.at[3, k], sem, (zz * NX + j, self.m))
 
-    def hop1(self, k, planes=(4, 3, 2, 1)):
+    def hop1(self, k, planes=(4, 3, 2, 1), sides=(0, 1)):
         for i, way, to in self.ways():
+            if i not in sides:
+                continue
             for n, place in ((4, pl.ds(0, 2)), (3, pl.ds(2, 4)), (2, pl.ds(6, 4))):
                 if n in planes:
                     zz, part = (self.off(4), pl.ds(2 * i, 2)) if n == 4 else (self.off(n * way), ALL)
@@ -360,10 +362,14 @@
 
         lax.fori_loop(0, B // T, back, 0)
 
-    for n in (4, 3, 2, 1):
-        produce(*sorted({n, NZ - n}))
-        for k in range(C):
-            ring3.hop1(k, (n,))
+    produce(4)
+    for k in range(C):
+        ring3.hop1(k, (4,))
+    for n in (3, 2, 1):
+        for side, shift in enumerate((n, NZ - n)):
+            produce(shift)
+            for k in range(C):
+                ring3.hop1(k, (n,), (side,))
     produce(0)
     for k in range(C):
         ring3.along_x(k)

time: 206 us -> 208 us (level)
  no operation moved by 1% of the time
where the time goes in v4:
time: 208 us; the launch traced here: 207 us
  Pallas kernels  205 us (99%)
    pallas_call x1, Pallas kernels, per_device(): pl.pallas_call(kernel, out_shape=vmem(S, Q, B), in_specs=[whole, pl.Block...  205 us

profile of v4, /device:TPU:8, one launch (start us, length us, event | category | flops | bytes accessed | tf_op | source)
XLA Modules:
  0.0 206.8 jit_solution(7547120943800502561)
XLA Ops:
  0.0 205.4 %soap_step.1 = bf16[4,256,1024]{2,1,0:T(8,128)(2,1)S(1)} custom-call(bf16[4,256,1024]{2,1,0:T(8,128)(2,1)} %grad.1, s32[256]{0:T(256)} %owners.1, bf16[1,1024,1024]{2,1,0:T(8,128)(2,1)} %left.1, bf16[1,1024,1024]{2,1,0:T(8,128)(2,1)} %right.1, bf16[1,1024,1024]{2,1,0:T(8,128)(2,1)} %first.1, bf16[1,1024,1024]{2,1,0:T(8,128)(2,1)} %second.1), custom_call_target="tpu_custom_call" | custom-call | flops 8589934592 | bytes 14680064 | tf_op jit(solution)/shard_map/soap_step/pallas_call | solution.py:417
  205.5 1.3 copy.8
